TPU v7x, 32 devices: a whole 2x2x4 slice. The times are simulated.
32 devices in a mesh: groups: 2 (over x), dp: 16 (over z, y, core).
Axes of the slice: x: 2, y: 2, z: 4, core: 2. Of those that a mesh axis runs over, the one named last changes fastest.
Arguments:
- tokens: bfloat16 [2048, 3072], P(('groups', 'dp')), parts along dimension 0, may hold values from -6 to 6
- router: bfloat16 [3072, 4], replicated, may hold values from -0.109375 to 0.109375
- routes: int32 [2048, 2], P(('groups', 'dp')), parts along dimension 0, may hold values from 0 to 3, all different within a row; in each aligned block of 64 rows (0 to 63, 64 to 127, ...) at most 36 rows name the same one
- w_gate: bfloat16 [3072, 32768], P(None, 'dp'), may hold values from -0.109375 to 0.109375
- w_up: bfloat16 [3072, 32768], P(None, 'dp'), may hold values from -0.109375 to 0.109375
- w_down: bfloat16 [32768, 3072], P('dp'), may hold values from -0.0625 to 0.0625
Outputs:
- mixed: bfloat16 [2048, 3072], P(('groups', 'dp')), parts along dimension 0
There are 2 independent parts, one for each index of `groups`. A program takes and returns all parts, laid end to end along the dimension named above; an argument that names none is the same for every part. Nothing has to cross between parts.
Inputs may be any that keep to these rules, and one draw needn't show every extreme that they name: `routes`: each token names 2 different experts; within the rows of one device no expert is named by more than 36 rows, a bound that some block reaches.
All inputs are finite; a program needn't handle non-finite values.
Results may differ from a plain program's by a relative error of at most 0.0058.
Values may be sent and summed in bfloat16 or wider, within the bound.
A program may use at most 128 MiB of HBM per device.

v0:
```python
import jax
import jax.numpy as jnp
from jax import lax
from jax.sharding import PartitionSpec as P

CAP = 36


def expert_partial(arrived, w_gate, w_up, w_down):
    dims_in = arrived.shape
    flat_rows = arrived.reshape(-1, dims_in[-1])
    gate_vals = jnp.dot(flat_rows, w_gate, preferred_element_type=jnp.float32)
    up_vals = jnp.dot(flat_rows, w_up, preferred_element_type=jnp.float32)
    hidden = (jax.nn.silu(gate_vals) * up_vals).astype(jnp.bfloat16)
    output = jnp.dot(hidden, w_down, preferred_element_type=jnp.float32).astype(jnp.bfloat16)
    return output.reshape(dims_in[:-1] + (w_down.shape[1],))


def local(tokens, router, routes, w_gate, w_up, w_down):
    tok_rows, width = tokens.shape
    experts = router.shape[1]
    top_count = routes.shape[1]
    devices_dp = lax.axis_size("dp")
    members = devices_dp // experts
    logits = jnp.dot(tokens, router, preferred_element_type=jnp.float32)
    onehot = routes[:, :, None] == jnp.arange(experts, dtype=jnp.int32)[None, None, :]
    picked = jnp.sum(jnp.where(onehot, logits[:, None, :], 0.0), axis=2)
    first_share = jax.nn.sigmoid(picked[:, 0] - picked[:, 1])
    shares = jnp.stack([first_share, 1.0 - first_share], axis=1)
    flat_hot = onehot.reshape(tok_rows * top_count, experts).astype(jnp.int32)
    before = jnp.cumsum(flat_hot, axis=0) - flat_hot
    slot_index = jnp.sum(before * flat_hot, axis=1)
    target = routes.reshape(-1) * CAP + slot_index
    select = target[None, :] == jnp.arange(experts * CAP, dtype=jnp.int32)[:, None]
    repeated = jnp.repeat(tokens, top_count, axis=0)
    packed = jnp.dot(select.astype(jnp.bfloat16), repeated, preferred_element_type=jnp.float32)
    packed = packed.astype(jnp.bfloat16).reshape(experts, CAP, width)
    outgoing = jnp.repeat(packed, members, axis=0)
    partial_value = expert_partial(
        lax.all_to_all(outgoing, "dp", split_axis=0, concat_axis=0, tiled=True),
        w_gate,
        w_up,
        w_down,
    )
    returned = lax.all_to_all(partial_value, "dp", split_axis=0, concat_axis=0, tiled=True)
    summed = returned.astype(jnp.float32).reshape(experts, members, CAP, width).sum(axis=1)
    flat_back = summed.reshape(experts * CAP, width)
    gathered = jnp.dot(select.astype(jnp.float32).T, flat_back, precision=lax.Precision.HIGHEST)
    weighted = gathered.reshape(tok_rows, top_count, width) * shares[:, :, None]
    return jnp.sum(weighted, axis=1).astype(jnp.bfloat16)


def solution(mesh):
    placed = (
        P(("groups", "dp"), None),
        P(),
        P(("groups", "dp"), None),
        P(None, "dp"),
        P(None, "dp"),
        P("dp", None),
    )
    return jax.shard_map(
        local, mesh=mesh, in_specs=placed, out_specs=P(("groups", "dp"), None), check_vma=False
    )
```

profile of v0, /device:TPU:15, one launch (start us, length us, event | category | flops | bytes accessed | tf_op | source)
XLA Modules:
  0.0 247.1 jit_solution(15363028632651862700)
XLA Ops:
  0.0 0.0 copy-start
  0.0 0.8 copy.23
  0.8 0.1 reshape.60
  0.9 0.1 fusion.5
  1.0 0.2 reduce_window_sum.11
  1.2 0.2 select_reduce_fusion
  1.4 1.4 broadcast_in_dim.24
  2.8 0.3 reshape.61
  3.1 0.4 convolution_convert_fusion.1
  3.5 0.2 reshape.62
  3.7 0.5 broadcast_in_dim.25
  4.2 93.1 %all_to_all.10 = bf16[16,36,3072]{2,1,0:T(8,128)(2,1)} all-to-all(bf16[16,36,3072]{2,1,0:T(8,128)(2,1)S(1)} %bitcast.16), channel_id=1, replica_groups=mesh['groups'=2,'dp'=16] {'dp'}, dimensions={0} | all-to-all | bytes 7077888 | tf_op jit(solution)/shard_map/all_to_all | solution.py:40
  97.3 4.7 %reshape.64 = bf16[576,3072]{1,0:T(8,128)(2,1)} reshape(bf16[16,36,3072]{2,1,0:T(8,128)(2,1)} %all_to_all.10) | data formatting | bytes 7077888 | tf_op jit(solution)/shard_map/reshape | solution.py:11
  101.9 12.9 %fusion.8 = f32[576,2048]{1,0:T(8,128)} fusion(bf16[576,3072]{1,0:T(8,128)(2,1)} %reshape.64, bf16[3072,2048]{1,0:T(8,128)(2,1)} %param.9), kind=kOutput, calls=%fused_computation.23 | convolution fusion | flops 7247757312 | bytes 20840448 | tf_op jit(solution)/shard_map/dot_general | solution.py:12
  114.8 27.2 %convolution_convert_fusion = bf16[576,3072]{1,0:T(8,128)(2,1)} fusion(bf16[2048,3072]{1,0:T(8,128)(2,1)} %param.11, f32[576,2048]{1,0:T(8,128)} %fusion.8, bf16[576,3072]{1,0:T(8,128)(2,1)} %reshape.64, bf16[3072,2048]{1,0:T(8,128)(2,1)} %param.10), kind=kOutput, calls=%fused_computation.2 | convolution fusion | flops 14504361984 | bytes 36962304 | tf_op jit(solution)/shard_map/dot_general | solution.py:15
  142.1 4.7 %reshape.65 = bf16[16,36,3072]{2,1,0:T(8,128)(2,1)} reshape(bf16[576,3072]{1,0:T(8,128)(2,1)} %convolution_convert_fusion) | data formatting | bytes 7077888 | tf_op jit(solution)/shard_map/reshape | solution.py:16
  146.7 0.0 copy-start.1
  146.8 0.0 copy-start.2
  146.8 5.6 %all-to-all-start.1 = ((bf16[16,36,3072]{2,1,0:T(8,128)(2,1)}), bf16[16,36,3072]{2,1,0:T(8,128)(2,1)}, u32[]{:S(2)}, u32[]{:S(2)}) async-start(bf16[16,36,3072]{2,1,0:T(8,128)(2,1)} %reshape.65), calls=%async_computation.1 | async-start | bytes 7864320 | tf_op jit(solution)/shard_map/all_to_all | solution.py:45
  152.3 0.1 reduce_sum.39
  152.5 0.1 copy.24
  152.6 0.0 copy-done
  152.6 0.0 copy-done.1
  152.6 0.2 fusion.9
  152.8 0.0 copy-done.2
  152.9 86.4 %all-to-all-done.1 = bf16[16,36,3072]{2,1,0:T(8,128)(2,1)} async-done(((bf16[16,36,3072]{2,1,0:T(8,128)(2,1)}), bf16[16,36,3072]{2,1,0:T(8,128)(2,1)}, u32[]{:S(2)}, u32[]{:S(2)}) %all-to-all-start.1) | async-done | bytes 3538976 | tf_op jit(solution)/shard_map/all_to_all | solution.py:45
  239.2 3.1 %convert_reduce_fusion = f32[4,36,3072]{2,1,0:T(8,128)S(1)} fusion(bf16[16,36,3072]{2,1,0:T(8,128)(2,1)} %all-to-all-done.1), kind=kLoop, calls=%fused_computation | loop fusion | flops 3096576 | bytes 5308416 | tf_op jit(solution)/shard_map/reduce_sum | solution.py:46
  242.3 1.4 reshape.71
  243.7 3.4 %fusion.1 = bf16[64,3072]{1,0:T(8,128)(2,1)} fusion(f32[144,3072,1]{1,0,2:T(8,128)} %reshape.71, f32[64,2]{0,1:T(2,128)S(1)} %pad_maximum_fusion, s32[64,2]{0,1:T(2,128)S(1)} %multiply_add_fusion), kind=kOutput, calls=%fused_computation.6 | convolution fusion | flops 680085504 | bytes 2163712 | tf_op jit(solution)/shard_map/dot_general | solution.py:48
  (5 shorter events, 0.1 us)
Async XLA Ops:
  0.0 152.6 %copy-start = (bf16[3072,4]{0,1:T(4,128)(2,1)S(1)}, bf16[3072,4]{0,1:T(4,128)(2,1)}, u32[]{:S(2)}) copy-start(bf16[3072,4]{0,1:T(4,128)(2,1)} %param.7) | copy-start | bytes 73732
  146.7 5.8 %copy-start.1 = (bf16[64,3072]{1,0:T(8,128)(2,1)S(1)}, bf16[64,3072]{1,0:T(8,128)(2,1)}, u32[]{:S(2)}) copy-start(bf16[64,3072]{1,0:T(8,128)(2,1)} %param.6) | copy-start | bytes 1179652
  146.8 6.0 %copy-start.2 = (s32[64,2]{0,1:T(2,128)S(1)}, s32[64,2]{0,1:T(2,128)}, u32[]{:S(2)}) copy-start(s32[64,2]{0,1:T(2,128)} %param.8) | copy-start | bytes 1540
  146.8 92.5 %all-to-all-start.1 = ((bf16[16,36,3072]{2,1,0:T(8,128)(2,1)}), bf16[16,36,3072]{2,1,0:T(8,128)(2,1)}, u32[]{:S(2)}, u32[]{:S(2)}) async-start(bf16[16,36,3072]{2,1,0:T(8,128)(2,1)} %reshape.65), calls=%async_computation.1 | async-start | bytes 7864320 | tf_op jit(solution)/shard_map/all_to_all | solution.py:45
where the time goes:
time: 248 us; the launch traced here: 247 us
  blocking collectives  93.1 us (38%)
  waiting for transfers between devices  86.4 us (35%)
  matrix products  44.2 us (18%)
  local copies, waits for them, and re-layouts  14.2 us (6%)
  starting transfers between devices  5.59 us (2%)
  other arithmetic  3.61 us (1%)
    all_to_all x1, blocking collectives, local(): lax.all_to_all(outgoing, 'dp', split_axis=0, concat_axis=0, tiled=True)  93.1 us
    all_to_all x1, waiting for transfers between devices, local(): lax.all_to_all(partial_value, 'dp', split_axis=0, concat_axis=0, tiled=True)  86.4 us
    dot_general x1, matrix products, expert_partial(): jnp.dot(hidden, w_down, preferred_element_type=jnp.float32)  27.2 us
    dot_general x1, matrix products, expert_partial(): gate_vals = jnp.dot(flat_rows, w_gate, preferred_element_type=jnp.float32)  12.9 us
    all_to_all x1, starting transfers between devices, local(): lax.all_to_all(partial_value, 'dp', split_axis=0, concat_axis=0, tiled=True)  5.59 us
  transfers between devices with their start and end apart: 1, of which 1 were waited for; matrix products, arithmetic and copies ran while one was open for 0% of the time, Pallas kernels for 0%

commit v1 on v0

v1 whole, which is shorter than its diff:
```python
import functools

import jax
import jax.numpy as jnp
from jax import lax
from jax.experimental import pallas as pl
from jax.experimental.pallas import tpu as pltpu
from jax.sharding import PartitionSpec as P

CAP = 36
MAIN = 32
TAIL = CAP - MAIN
PIECES = 16 // TAIL
MESH = pl.DeviceIdType.MESH
TILE = 256


def moe_kernel(experts, chips, pa, pb, wg_hbm, wu_hbm, wd_hbm, ra, rb,
               wg, wu, wd, xf, xb, hid, cra, crb, yra, yrb, zsa, zsb,
               load_sem, own_sem, z_send, z_recv, y_send, y_recv, c_send, c_recv,
               rc_send, rc_recv, ry_send, ry_recv, rz_send, rz_recv):
    members = 2 * chips
    width = pa.shape[-1]
    piece = width // PIECES
    main_rows, tail_rows = members * MAIN, members * TAIL
    group = lax.axis_index("groups")
    me = lax.axis_index("dp")
    mine = lax.div(me, members)
    member = lax.rem(me, members)
    chip, core = lax.div(member, 2), lax.rem(member, 2)
    other = 1 - core

    def device(expert, chip_at, core_at):
        return (group, expert * members + chip_at * 2 + core_at)

    def expert_at(step):
        return lax.rem(mine + step, experts)

    def expert_before(step):
        return lax.rem(mine - step + experts, experts)

    def rows(core_at, chip_at, size, count):
        return pl.ds(pl.multiple_of((core_at * chips + chip_at) * size, size), count * size)

    loads = []
    for i, (src, dst) in enumerate(((wg_hbm, wg), (wu_hbm, wu), (wd_hbm, wd))):
        load = pltpu.make_async_copy(src, dst, load_sem.at[i])
        load.start()
        loads.append(load)
    own = [
        pltpu.make_async_copy(pa.at[mine], xf.at[mine, rows(core, chip, MAIN, 1)], own_sem.at[0]),
        pltpu.make_async_copy(pb.at[mine], xb.at[mine, rows(core, chip, 16, 1)], own_sem.at[1]),
    ]
    for copy in own:
        copy.start()

    partner = device(mine, chip, other)
    barrier = pltpu.get_barrier_semaphore()
    peers = [device(expert_at(s), chip, core) for s in range(1, experts)]
    peers += [device(mine, lax.rem(chip + d, chips), core) for d in range(1, chips)]
    peers += [partner]
    for peer in peers:
        pl.semaphore_signal(barrier, inc=1, device_id=peer, device_id_type=MESH)
    pl.semaphore_wait(barrier, len(peers))

    def send(pairs, sends, recvs, index, target):
        made = []
        for i, (src, dst) in enumerate(pairs):
            copy = pltpu.make_async_remote_copy(
                src_ref=src, dst_ref=dst, send_sem=sends.at[index, i], recv_sem=recvs.at[index, i],
                device_id=target, device_id_type=MESH)
            copy.start()
            made.append(copy)
        return made

    def arrive(copies):
        for copy in copies:
            copy.wait_recv()

    def sent(copies):
        for copy in copies:
            copy.wait_send()

    pending = []
    z_copies = {}
    for s in range(1, experts):
        to = expert_before(s)
        z_copies[s] = send(
            ((pa.at[to], xf.at[mine, rows(core, chip, MAIN, 1)]),
             (pb.at[to], xb.at[mine, rows(core, chip, 16, 1)])),
            z_send, z_recv, s, device(to, chip, core))
        pending += z_copies[s]

    y_copies, c_copies = {}, {}

    def spread(s):
        at = expert_at(s)
        if s == 0:
            for copy in own:
                copy.wait()
        else:
            arrive(z_copies[s])
        y_copies[s] = []
        for d in range(1, chips):
            a_ref = xf.at[at, rows(core, chip, MAIN, 1)]
            b_ref = xb.at[at, rows(core, chip, 16, 1)]
            y_copies[s] += send(((a_ref, a_ref), (b_ref, b_ref)), y_send, y_recv, s * chips + d,
                                device(mine, lax.rem(chip + d, chips), core))

    def forward(s):
        at = expert_at(s)
        arrive(y_copies[s])
        a_ref = xf.at[at, rows(core, 0, MAIN, chips)]
        b_ref = xb.at[at, rows(core, 0, 16, chips)]
        c_copies[s] = send(((a_ref, a_ref), (b_ref, b_ref)), c_send, c_recv, s, partner)

    out_rows = lax.broadcasted_iota(jnp.int32, (tail_rows, members * 16), 0)
    in_rows = lax.broadcasted_iota(jnp.int32, (tail_rows, members * 16), 1)
    back_out = lax.broadcasted_iota(jnp.int32, (members * 16, tail_rows), 0)
    back_in = lax.broadcasted_iota(jnp.int32, (members * 16, tail_rows), 1)

    def compute(s):
        at = expert_at(s)
        arrive(c_copies[s])
        sent(y_copies[s])
        sent(c_copies[s])
        for q in range(PIECES):
            pick = (in_rows == (out_rows // TAIL) * 16 + q * TAIL + out_rows % TAIL)
            moved = jnp.dot(pick.astype(jnp.bfloat16), xb[at], preferred_element_type=jnp.float32)
            xf[at, main_rows:main_rows + tail_rows, q * piece:(q + 1) * piece] = moved.astype(jnp.bfloat16)
        if s == 0:
            loads[0].wait()
            loads[1].wait()

        @pl.loop(0, hid.shape[1] // TILE)
        def _(j):
            cols = pl.ds(pl.multiple_of(j * TILE, TILE), TILE)
            gate = jnp.dot(xf[at], wg[:, cols], preferred_element_type=jnp.float32)
            up = jnp.dot(xf[at], wu[:, cols], preferred_element_type=jnp.float32)
            hid[:, cols] = (gate / (1.0 + jnp.exp(-gate)) * up).astype(jnp.bfloat16)

        if s == 0:
            loads[2].wait()

        @pl.loop(0, width // TILE)
        def _(j):
            cols = pl.ds(pl.multiple_of(j * TILE, TILE), TILE)
            xf[at, :, cols] = jnp.dot(hid[...], wd[:, cols], preferred_element_type=jnp.float32).astype(jnp.bfloat16)

        total = jnp.zeros((members * 16, piece), jnp.float32)
        for q in range(PIECES):
            place = (back_out == (back_in // TAIL) * 16 + q * TAIL + back_in % TAIL)
            total = total + jnp.dot(
                place.astype(jnp.bfloat16),
                xf[at, main_rows:main_rows + tail_rows, q * piece:(q + 1) * piece],
                preferred_element_type=jnp.float32)
        xb[at] = total.astype(jnp.bfloat16)

    rc_copies, ry_copies, rz_copies = {}, {}, {}

    def pair(s):
        at = expert_at(s)
        rc_copies[s] = send(
            ((xf.at[at, rows(other, 0, MAIN, chips)], cra.at[s]),
             (xb.at[at, rows(other, 0, 16, chips)], crb.at[s])),
            rc_send, rc_recv, s, partner)
        pending.extend(rc_copies[s])

    def across(s):
        at = expert_at(s)
        arrive(rc_copies[s])
        cra[s] = (cra[s].astype(jnp.float32)
                  + xf[at, rows(core, 0, MAIN, chips)].astype(jnp.float32)).astype(jnp.bfloat16)
        crb[s] = (crb[s].astype(jnp.float32)
                  + xb[at, rows(core, 0, 16, chips)].astype(jnp.float32)).astype(jnp.bfloat16)
        ry_copies[s] = []
        for d in range(1, chips):
            to = lax.rem(chip + d, chips)
            ry_copies[s] += send(
                ((cra.at[s, rows(0, to, MAIN, 1)], yra.at[s, d - 1]),
                 (crb.at[s, rows(0, to, 16, 1)], yrb.at[s, d - 1])),
                ry_send, ry_recv, s * chips + d, device(mine, to, core))
        pending.extend(ry_copies[s])

    def home(s):
        arrive(ry_copies[s])
        a_sum = cra[s, rows(0, chip, MAIN, 1)].astype(jnp.float32)
        b_sum = crb[s, rows(0, chip, 16, 1)].astype(jnp.float32)
        for d in range(1, chips):
            a_sum = a_sum + yra[s, d - 1].astype(jnp.float32)
            b_sum = b_sum + yrb[s, d - 1].astype(jnp.float32)
        if s == 0:
            ra[mine] = a_sum.astype(jnp.bfloat16)
            rb[mine] = b_sum.astype(jnp.bfloat16)
            return
        zsa[s] = a_sum.astype(jnp.bfloat16)
        zsb[s] = b_sum.astype(jnp.bfloat16)
        rz_copies[s] = send(((zsa.at[s], ra.at[mine]), (zsb.at[s], rb.at[mine])),
                            rz_send, rz_recv, s, device(expert_at(s), chip, core))
        pending.extend(rz_copies[s])

    spread(0)
    for s in range(experts):
        if s + 1 < experts:
            spread(s + 1)
        if s == 0:
            forward(0)
        compute(s)
        pair(s)
        if s + 1 < experts:
            forward(s + 1)
        if s >= 1:
            home(s - 1)
        across(s)
    home(experts - 1)
    for s in range(1, experts):
        arrive(rz_copies[s])
    sent(pending)


def exchange(packed_a, packed_b, w_gate, w_up, w_down, devices_dp):
    experts, _, width = packed_a.shape
    members = devices_dp // experts
    chips = members // 2
    piece = width // PIECES
    hidden = w_gate.shape[1]
    bf16 = jnp.bfloat16
    dma = pltpu.SemaphoreType.DMA
    vmem = pl.BlockSpec(memory_space=pltpu.VMEM)
    hbm = pl.BlockSpec(memory_space=pl.ANY)
    flops = experts * members * CAP * width * hidden * 6
    return pl.pallas_call(
        functools.partial(moe_kernel, experts, chips),
        out_shape=[jax.ShapeDtypeStruct((experts, MAIN, width), bf16),
                   jax.ShapeDtypeStruct((experts, 16, piece), bf16)],
        in_specs=[vmem, vmem, hbm, hbm, hbm],
        out_specs=[vmem, vmem],
        scratch_shapes=[
            pltpu.VMEM(w_gate.shape, bf16),
            pltpu.VMEM(w_up.shape, bf16),
            pltpu.VMEM(w_down.shape, bf16),
            pltpu.VMEM((experts, members * CAP, width), bf16),
            pltpu.VMEM((experts, members * 16, piece), bf16),
            pltpu.VMEM((members * CAP, hidden), bf16),
            pltpu.VMEM((experts, chips * MAIN, width), bf16),
            pltpu.VMEM((experts, chips * 16, piece), bf16),
            pltpu.VMEM((experts, chips - 1, MAIN, width), bf16),
            pltpu.VMEM((experts, chips - 1, 16, piece), bf16),
            pltpu.VMEM((experts, MAIN, width), bf16),
            pltpu.VMEM((experts, 16, piece), bf16),
            dma((3,)),
            dma((2,)),
            dma((experts, 2)), dma((experts, 2)),
            dma((experts * chips, 2)), dma((experts * chips, 2)),
            dma((experts, 2)), dma((experts, 2)),
            dma((experts, 2)), dma((experts, 2)),
            dma((experts * chips, 2)), dma((experts * chips, 2)),
            dma((experts, 2)), dma((experts, 2)),
        ],
        compiler_params=pltpu.CompilerParams(
            collective_id=0, has_side_effects=True, vmem_limit_bytes=60 * 1024 * 1024),
        cost_estimate=pl.CostEstimate(
            flops=flops, bytes_accessed=6 * width * hidden, transcendentals=0),
    )(packed_a, packed_b, w_gate, w_up, w_down)


def local(tokens, router, routes, w_gate, w_up, w_down):
    tok_rows, width = tokens.shape
    experts = router.shape[1]
    top_count = routes.shape[1]
    devices_dp = lax.axis_size("dp")
    logits = jnp.dot(tokens, router, preferred_element_type=jnp.float32)
    onehot = routes[:, :, None] == jnp.arange(experts, dtype=jnp.int32)[None, None, :]
    picked = jnp.sum(jnp.where(onehot, logits[:, None, :], 0.0), axis=2)
    first_share = jax.nn.sigmoid(picked[:, 0] - picked[:, 1])
    shares = jnp.stack([first_share, 1.0 - first_share], axis=1)
    flat_hot = onehot.reshape(tok_rows * top_count, experts).astype(jnp.int32)
    before = jnp.cumsum(flat_hot, axis=0) - flat_hot
    slot_index = jnp.sum(before * flat_hot, axis=1)
    target = routes.reshape(-1) * CAP + slot_index
    select = target[None, :] == jnp.arange(experts * CAP, dtype=jnp.int32)[:, None]
    by_token = select.reshape(experts * CAP, tok_rows, top_count)
    token_select = jnp.any(by_token, axis=2)
    packed = jnp.dot(token_select.astype(jnp.bfloat16), tokens, preferred_element_type=jnp.float32)
    packed = packed.astype(jnp.bfloat16).reshape(experts, CAP, width)
    piece = width // PIECES
    tail = packed[:, MAIN:].reshape(experts, TAIL, PIECES, piece).transpose(0, 2, 1, 3)
    back_a, back_b = exchange(packed[:, :MAIN], tail.reshape(experts, 16, piece), w_gate, w_up, w_down, devices_dp)
    back_tail = back_b.reshape(experts, PIECES, TAIL, piece).transpose(0, 2, 1, 3).reshape(experts, TAIL, width)
    flat_back = jnp.concatenate([back_a, back_tail], axis=1).reshape(experts * CAP, width)
    weights = jnp.sum(jnp.where(by_token, shares[None], 0.0), axis=2)
    mixed = jnp.dot(weights.T, flat_back.astype(jnp.float32), precision=lax.Precision.HIGHEST)
    return mixed.astype(jnp.bfloat16)


def solution(mesh):
    placed = (
        P(("groups", "dp"), None),
        P(),
        P(("groups", "dp"), None),
        P(None, "dp"),
        P(None, "dp"),
        P("dp", None),
    )
    return jax.shard_map(
        local, mesh=mesh, in_specs=placed, out_specs=P(("groups", "dp"), None), check_vma=False
    )
```

time: 248 us -> 97.6 us (0.39)
  the two profiles are of different devices: /device:TPU:15 before, /device:TPU:0 now
where the time goes in v1:
time: 97.6 us; the launch traced here: 97.4 us
  Pallas kernels  88.6 us (91%)
  local copies, waits for them, and re-layouts  4.09 us (4%)
  other arithmetic  2.62 us (3%)
  matrix products  1.88 us (2%)
    pallas_call x1, Pallas kernels, exchange(): pl.pallas_call(functools.partial(moe_kernel, experts, chips), out_shape=[...  88.6 us

profile of v1, /device:TPU:0, one launch (start us, length us, event | category | flops | bytes accessed | tf_op | source)
XLA Modules:
  0.0 97.4 jit_solution(5043095388591634915)
XLA Ops:
  0.0 0.0 copy-start
  0.0 0.8 copy.31
  0.8 0.1 eq.36
  1.0 0.1 fusion.1
  1.1 0.2 reduce_window_sum.11
  1.2 0.2 select_reduce_fusion.1
  1.4 0.1 reduce_sum.30
  1.6 0.1 copy.32
  1.6 0.7 multiply_add_fusion
  2.3 0.1 fusion
  2.4 0.0 copy-done
  2.4 0.4 convolution_convert_fusion
  2.9 0.2 reshape.42
  3.0 0.9 slice.16.pa
  4.0 0.7 reshape.44.pb
  4.7 88.6 %shard_map.64 = (bf16[4,32,3072]{2,1,0:T(8,128)(2,1)}, bf16[4,16,768]{2,1,0:T(8,128)(2,1)}) custom-call(bf16[4,32,3072]{2,1,0:T(8,128)(2,1)} %slice.16.pa, bf16[4,16,768]{2,1,0:T(8,128)(2,1)} %reshape.44.pb, bf16[3072,2048]{1,0:T(8,128)(2,1)} %wg_hbm.1, bf16[3072,2048]{1,0:T(8,128)(2,1)} %wu_hbm.1, bf16[2048,3072]{1,0:T(8,128)(2,1)} %wd_hbm.1), custom_call_target="tpu_custom_call" | custom-call | flops 21743271936 | bytes 37748736 | tf_op jit(solution)/shard_map/pallas_call | solution.py:232
  93.3 0.0 copy-start.1
  93.3 0.9 reshape.45
  94.3 0.0 copy-start.2
  94.3 1.2 %pad_maximum_fusion = bf16[4,36,3072]{2,1,0:T(8,128)(2,1)S(1)} fusion(bf16[4,4,3072]{2,1,0:T(4,128)(2,1)S(1)} %bitcast.12, bf16[4,32,3072]{2,1,0:T(8,128)(2,1)} %get-tuple-element.7), kind=kLoop, calls=%fused_computation.2 | loop fusion | flops 1769472 | bytes 1769472 | tf_op jit(solution)/shard_map/concatenate | solution.py:290
  95.5 0.2 reshape.47
  95.7 0.0 copy-done.1
  95.7 0.2 fusion.2
  95.9 0.0 copy-done.2
  96.0 0.1 select_reduce_fusion
  96.1 1.3 %convolution_convert_fusion.1 = bf16[64,3072]{1,0:T(8,128)(2,1)} fusion(f32[144,64]{0,1:T(8,128)S(1)} %select_reduce_fusion, bf16[144,3072]{1,0:T(8,128)(2,1)S(1)} %reshape.47), kind=kOutput, calls=%fused_computation.1 | convolution fusion | flops 339935232 | bytes 1314816 | tf_op jit(solution)/shard_map/dot_general | solution.py:292
  (4 shorter events, 0.1 us)
Async XLA Ops:
  0.0 2.4 %copy-start = (bf16[64,3072]{1,0:T(8,128)(2,1)S(1)}, bf16[64,3072]{1,0:T(8,128)(2,1)}, u32[]{:S(2)}) copy-start(bf16[64,3072]{1,0:T(8,128)(2,1)} %param.6) | copy-start | bytes 1179652
  93.3 2.4 %copy-start.1 = (bf16[3072,4]{0,1:T(4,128)(2,1)S(1)}, bf16[3072,4]{0,1:T(4,128)(2,1)}, u32[]{:S(2)}) copy-start(bf16[3072,4]{0,1:T(4,128)(2,1)} %param.7) | copy-start | bytes 73732
  94.3 1.7 %copy-start.2 = (s32[64,2]{0,1:T(2,128)S(1)}, s32[64,2]{0,1:T(2,128)}, u32[]{:S(2)}) copy-start(s32[64,2]{0,1:T(2,128)} %param.8) | copy-start | bytes 1540

commit v2 on v1

--- a/solution.py
+++ b/solution.py
@@ -12,11 +12,11 @@
 TAIL = CAP - MAIN
 PIECES = 16 // TAIL
 MESH = pl.DeviceIdType.MESH
-TILE = 256
-
-
-def moe_kernel(experts, chips, pa, pb, wg_hbm, wu_hbm, wd_hbm, ra, rb,
-               wg, wu, wd, xf, xb, hid, cra, crb, yra, yrb, zsa, zsb,
+TILE = 512
+
+
+def moe_kernel(experts, chips, tokens, routes, router, wg_hbm, wu_hbm, wd_hbm, mixed,
+               pa, pb, ra, rb, wg, wu, wd, xf, xb, hid, cra, crb, yra, yrb, zsa, zsb,
                load_sem, own_sem, z_send, z_recv, y_send, y_recv, c_send, c_recv,
                rc_send, rc_recv, ry_send, ry_recv, rz_send, rz_recv):
     members = 2 * chips
@@ -42,17 +42,23 @@
     def rows(core_at, chip_at, size, count):
         return pl.ds(pl.multiple_of((core_at * chips + chip_at) * size, size), count * size)
 
-    loads = []
-    for i, (src, dst) in enumerate(((wg_hbm, wg), (wu_hbm, wu), (wd_hbm, wd))):
-        load = pltpu.make_async_copy(src, dst, load_sem.at[i])
-        load.start()
-        loads.append(load)
-    own = [
-        pltpu.make_async_copy(pa.at[mine], xf.at[mine, rows(core, chip, MAIN, 1)], own_sem.at[0]),
-        pltpu.make_async_copy(pb.at[mine], xb.at[mine, rows(core, chip, 16, 1)], own_sem.at[1]),
-    ]
-    for copy in own:
-        copy.start()
+    hidden = hid.shape[1]
+    step_cols = min(TILE, hidden)
+    steps = hidden // step_cols
+
+    def cols_at(j, size):
+        return pl.ds(pl.multiple_of(j * size, size), size)
+
+    def load_in(j):
+        cols = cols_at(j, step_cols)
+        return [pltpu.make_async_copy(wg_hbm.at[:, cols], wg.at[:, cols], load_sem.at[2 * j]),
+                pltpu.make_async_copy(wu_hbm.at[:, cols], wu.at[:, cols], load_sem.at[2 * j + 1])]
+
+    load_down = pltpu.make_async_copy(wd_hbm, wd, load_sem.at[2 * steps])
+    for j in range(steps):
+        for load in load_in(j):
+            load.start()
+    load_down.start()
 
     partner = device(mine, chip, other)
     barrier = pltpu.get_barrier_semaphore()
@@ -61,6 +67,47 @@
     peers += [partner]
     for peer in peers:
         pl.semaphore_signal(barrier, inc=1, device_id=peer, device_id_type=MESH)
+
+    tok_rows = tokens.shape[0]
+    f32, bf16 = jnp.float32, jnp.bfloat16
+    first, second = routes[0:1, :], routes[1:2, :]
+    expert_row = lax.broadcasted_iota(jnp.int32, (experts, tok_rows), 0)
+    named = (expert_row == first) | (expert_row == second)
+    earlier = (lax.broadcasted_iota(jnp.int32, (tok_rows, tok_rows), 0)
+               < lax.broadcasted_iota(jnp.int32, (tok_rows, tok_rows), 1))
+    slot = jnp.dot(jnp.where(named, 1.0, 0.0).astype(bf16), jnp.where(earlier, 1.0, 0.0).astype(bf16),
+                   preferred_element_type=f32)
+    slot = jnp.where(named, slot, -1.0).astype(jnp.int32)
+    main_slot = lax.broadcasted_iota(jnp.int32, (MAIN, tok_rows), 0)
+    tail_slot = lax.broadcasted_iota(jnp.int32, (16, tok_rows), 0)
+
+    def main_values(values):
+        return jnp.concatenate(
+            [jnp.where(slot[e:e + 1, :] == main_slot, values[e:e + 1, :], 0.0) for e in range(experts)], axis=0)
+
+    def tail_values(values, q):
+        wanted = jnp.where(tail_slot // TAIL == q, MAIN + tail_slot % TAIL, -2)
+        return jnp.concatenate(
+            [jnp.where(slot[e:e + 1, :] == wanted, values[e:e + 1, :], 0.0) for e in range(experts)], axis=0)
+
+    ones = jnp.ones((experts, tok_rows), f32)
+    pick_main = main_values(ones).astype(bf16)
+    pick_tail = [tail_values(ones, q).astype(bf16) for q in range(PIECES)]
+    for j in range(PIECES):
+        cols = slice(j * piece, (j + 1) * piece)
+        block = jnp.dot(pick_main, tokens[:, cols], preferred_element_type=f32).astype(bf16)
+        pa[:, :, cols] = block.reshape(experts, MAIN, piece)
+    tails = jnp.zeros((experts * 16, piece), f32)
+    for q in range(PIECES):
+        tails = tails + jnp.dot(pick_tail[q], tokens[:, q * piece:(q + 1) * piece], preferred_element_type=f32)
+    pb[...] = tails.astype(bf16).reshape(experts, 16, piece)
+
+    own = [
+        pltpu.make_async_copy(pa.at[mine], xf.at[mine, rows(core, chip, MAIN, 1)], own_sem.at[0]),
+        pltpu.make_async_copy(pb.at[mine], xb.at[mine, rows(core, chip, 16, 1)], own_sem.at[1]),
+    ]
+    for copy in own:
+        copy.start()
     pl.semaphore_wait(barrier, len(peers))
 
     def send(pairs, sends, recvs, index, target):
@@ -83,13 +130,16 @@
 
     pending = []
     z_copies = {}
-    for s in range(1, experts):
+
+    def dispatch(s):
         to = expert_before(s)
+        if s > 1:
+            sent(z_copies[s - 1][:1])
         z_copies[s] = send(
             ((pa.at[to], xf.at[mine, rows(core, chip, MAIN, 1)]),
              (pb.at[to], xb.at[mine, rows(core, chip, 16, 1)])),
             z_send, z_recv, s, device(to, chip, core))
-        pending += z_copies[s]
+        pending.extend(z_copies[s] if s == experts - 1 else z_copies[s][1:])
 
     y_copies, c_copies = {}, {}
 
@@ -119,33 +169,38 @@
     back_out = lax.broadcasted_iota(jnp.int32, (members * 16, tail_rows), 0)
     back_in = lax.broadcasted_iota(jnp.int32, (members * 16, tail_rows), 1)
 
-    def compute(s):
-        at = expert_at(s)
-        arrive(c_copies[s])
+    def hidden_units(s, begin, end):
+        at = expert_at(s)
+        if begin == 0:
+            arrive(c_copies[s])
+            for q in range(PIECES):
+                pick = (in_rows == (out_rows // TAIL) * 16 + q * TAIL + out_rows % TAIL)
+                moved = jnp.dot(pick.astype(bf16), xb[at], preferred_element_type=f32)
+                xf[at, main_rows:main_rows + tail_rows, q * piece:(q + 1) * piece] = moved.astype(bf16)
+        if begin == end:
+            return
+
+        @pl.loop(begin, end)
+        def _(j):
+            if s == 0:
+                for load in load_in(j):
+                    load.wait()
+            cols = cols_at(j, step_cols)
+            gate = jnp.dot(xf[at], wg[:, cols], preferred_element_type=f32)
+            up = jnp.dot(xf[at], wu[:, cols], preferred_element_type=f32)
+            hid[:, cols] = (gate / (1.0 + jnp.exp(-gate)) * up).astype(bf16)
+
+    def down(s):
+        at = expert_at(s)
         sent(y_copies[s])
         sent(c_copies[s])
-        for q in range(PIECES):
-            pick = (in_rows == (out_rows // TAIL) * 16 + q * TAIL + out_rows % TAIL)
-            moved = jnp.dot(pick.astype(jnp.bfloat16), xb[at], preferred_element_type=jnp.float32)
-            xf[at, main_rows:main_rows + tail_rows, q * piece:(q + 1) * piece] = moved.astype(jnp.bfloat16)
         if s == 0:
-            loads[0].wait()
-            loads[1].wait()
-
-        @pl.loop(0, hid.shape[1] // TILE)
-        def _(j):
-            cols = pl.ds(pl.multiple_of(j * TILE, TILE), TILE)
-            gate = jnp.dot(xf[at], wg[:, cols], preferred_element_type=jnp.float32)
-            up = jnp.dot(xf[at], wu[:, cols], preferred_element_type=jnp.float32)
-            hid[:, cols] = (gate / (1.0 + jnp.exp(-gate)) * up).astype(jnp.bfloat16)
-
-        if s == 0:
-            loads[2].wait()
+            load_down.wait()
 
         @pl.loop(0, width // TILE)
         def _(j):
-            cols = pl.ds(pl.multiple_of(j * TILE, TILE), TILE)
-            xf[at, :, cols] = jnp.dot(hid[...], wd[:, cols], preferred_element_type=jnp.float32).astype(jnp.bfloat16)
+            cols = cols_at(j, TILE)
+            xf[at, :, cols] = jnp.dot(hid[...], wd[:, cols], preferred_element_type=f32).astype(bf16)
 
         total = jnp.zeros((members * 16, piece), jnp.float32)
         for q in range(PIECES):
@@ -199,27 +254,63 @@
                             rz_send, rz_recv, s, device(expert_at(s), chip, core))
         pending.extend(rz_copies[s])
 
+    dispatch(1)
     spread(0)
+    forward(0)
+    if experts > 2:
+        dispatch(2)
+    spread(1)
     for s in range(experts):
-        if s + 1 < experts:
-            spread(s + 1)
-        if s == 0:
-            forward(0)
-        compute(s)
-        pair(s)
+        hidden_units(s, 0, 1)
+        if s >= 1:
+            across(s - 1)
+        if s >= 2:
+            home(s - 2)
+        if steps > 1:
+            hidden_units(s, 1, steps)
         if s + 1 < experts:
             forward(s + 1)
-        if s >= 1:
-            home(s - 1)
-        across(s)
+        down(s)
+        pair(s)
+        if s + 3 < experts:
+            dispatch(s + 3)
+        if s + 2 < experts:
+            spread(s + 2)
+    home(experts - 2)
+    across(experts - 1)
+
+    logits = lax.dot_general(router[...], tokens[...], (((1,), (1,)), ((), ())), preferred_element_type=f32)
+    gap = jnp.sum(jnp.where(expert_row == first, logits, 0.0) - jnp.where(expert_row == second, logits, 0.0),
+                  axis=0, keepdims=True)
+    share = 1.0 / (1.0 + jnp.exp(-gap))
+    shares = jnp.where(expert_row == first, share, 1.0 - share)
+
+    def parts(values):
+        high = values.astype(bf16)
+        left = values - high.astype(f32)
+        middle = left.astype(bf16)
+        return high, middle, (left - middle.astype(f32)).astype(bf16)
+
+    def weighted(pieces, data):
+        return sum(lax.dot_general(p, data, (((0,), (0,)), ((), ())), preferred_element_type=f32) for p in pieces)
+
+    main_shares = parts(main_values(shares))
+    tail_shares = [parts(tail_values(shares, q)) for q in range(PIECES)]
     home(experts - 1)
     for s in range(1, experts):
         arrive(rz_copies[s])
+    tail_data = rb[...].reshape(experts * 16, piece)
+    for q in range(PIECES):
+        cols = slice(q * piece, (q + 1) * piece)
+        main_data = ra[:, :, cols].reshape(experts * MAIN, piece)
+        mixed[:, cols] = (weighted(main_shares, main_data) + weighted(tail_shares[q], tail_data)).astype(bf16)
     sent(pending)
 
 
-def exchange(packed_a, packed_b, w_gate, w_up, w_down, devices_dp):
-    experts, _, width = packed_a.shape
+def local(tokens, router, routes, w_gate, w_up, w_down):
+    tok_rows, width = tokens.shape
+    experts = router.shape[1]
+    devices_dp = lax.axis_size("dp")
     members = devices_dp // experts
     chips = members // 2
     piece = width // PIECES
@@ -231,11 +322,14 @@
     flops = experts * members * CAP * width * hidden * 6
     return pl.pallas_call(
         functools.partial(moe_kernel, experts, chips),
-        out_shape=[jax.ShapeDtypeStruct((experts, MAIN, width), bf16),
-                   jax.ShapeDtypeStruct((experts, 16, piece), bf16)],
-        in_specs=[vmem, vmem, hbm, hbm, hbm],
-        out_specs=[vmem, vmem],
+        out_shape=jax.ShapeDtypeStruct((tok_rows, width), bf16),
+        in_specs=[vmem, vmem, vmem, hbm, hbm, hbm],
+        out_specs=vmem,
         scratch_shapes=[
+            pltpu.VMEM((experts, MAIN, width), bf16),
+            pltpu.VMEM((experts, 16, piece), bf16),
+            pltpu.VMEM((experts, MAIN, width), bf16),
+            pltpu.VMEM((experts, 16, piece), bf16),
             pltpu.VMEM(w_gate.shape, bf16),
             pltpu.VMEM(w_up.shape, bf16),
             pltpu.VMEM(w_down.shape, bf16),
@@ -248,7 +342,7 @@
             pltpu.VMEM((experts, chips - 1, 16, piece), bf16),
             pltpu.VMEM((experts, MAIN, width), bf16),
             pltpu.VMEM((experts, 16, piece), bf16),
-            dma((3,)),
+            dma((2 * (hidden // min(TILE, hidden)) + 1,)),
             dma((2,)),
             dma((experts, 2)), dma((experts, 2)),
             dma((experts * chips, 2)), dma((experts * chips, 2)),
@@ -261,36 +355,7 @@
             collective_id=0, has_side_effects=True, vmem_limit_bytes=60 * 1024 * 1024),
         cost_estimate=pl.CostEstimate(
             flops=flops, bytes_accessed=6 * width * hidden, transcendentals=0),
-    )(packed_a, packed_b, w_gate, w_up, w_down)
-
-
-def local(tokens, router, routes, w_gate, w_up, w_down):
-    tok_rows, width = tokens.shape
-    experts = router.shape[1]
-    top_count = routes.shape[1]
-    devices_dp = lax.axis_size("dp")
-    logits = jnp.dot(tokens, router, preferred_element_type=jnp.float32)
-    onehot = routes[:, :, None] == jnp.arange(experts, dtype=jnp.int32)[None, None, :]
-    picked = jnp.sum(jnp.where(onehot, logits[:, None, :], 0.0), axis=2)
-    first_share = jax.nn.sigmoid(picked[:, 0] - picked[:, 1])
-    shares = jnp.stack([first_share, 1.0 - first_share], axis=1)
-    flat_hot = onehot.reshape(tok_rows * top_count, experts).astype(jnp.int32)
-    before = jnp.cumsum(flat_hot, axis=0) - flat_hot
-    slot_index = jnp.sum(before * flat_hot, axis=1)
-    target = routes.reshape(-1) * CAP + slot_index
-    select = target[None, :] == jnp.arange(experts * CAP, dtype=jnp.int32)[:, None]
-    by_token = select.reshape(experts * CAP, tok_rows, top_count)
-    token_select = jnp.any(by_token, axis=2)
-    packed = jnp.dot(token_select.astype(jnp.bfloat16), tokens, preferred_element_type=jnp.float32)
-    packed = packed.astype(jnp.bfloat16).reshape(experts, CAP, width)
-    piece = width // PIECES
-    tail = packed[:, MAIN:].reshape(experts, TAIL, PIECES, piece).transpose(0, 2, 1, 3)
-    back_a, back_b = exchange(packed[:, :MAIN], tail.reshape(experts, 16, piece), w_gate, w_up, w_down, devices_dp)
-    back_tail = back_b.reshape(experts, PIECES, TAIL, piece).transpose(0, 2, 1, 3).reshape(experts, TAIL, width)
-    flat_back = jnp.concatenate([back_a, back_tail], axis=1).reshape(experts * CAP, width)
-    weights = jnp.sum(jnp.where(by_token, shares[None], 0.0), axis=2)
-    mixed = jnp.dot(weights.T, flat_back.astype(jnp.float32), precision=lax.Precision.HIGHEST)
-    return mixed.astype(jnp.bfloat16)
+    )(tokens, routes.T, router.T, w_gate, w_up, w_down)
 
 
 def solution(mesh):

time: 97.6 us -> 72.2 us (0.74)
  Pallas kernels: 88.6 us -> 70.3 us
  other arithmetic: 2.62 us -> 0 us
  local copies, waits for them, and re-layouts: 4.09 us -> 1.77 us
  matrix products: 1.88 us -> 0 us
    pallas_call x1, Pallas kernels: 88.6 us -> 70.3 us  [local(): pl.pallas_call(functools.partial(moe_kernel, experts, chips), out_shape=j...]
    reshape x4 -> x0, local copies, waits for them, and re-layouts: 1.95 us -> none  [the longest x1 0.93 us: local(): back_b.reshape(experts, PIECES, TAIL, piece).transpose(0, 2, 1, 3)]
    dot_general x3 -> x0, matrix products: 1.88 us -> none  [the longest x1 1.26 us: local(): jnp.dot(weights.T, flat_back.astype(jnp.float32), precision=lax.Precision...]
    concatenate x1 -> x0, other arithmetic: 1.24 us -> none  [local(): jnp.concatenate([back_a, back_tail], axis=1).reshape(experts * CAP, width)]
where the time goes in v2:
time: 72.2 us; the launch traced here: 72.1 us
  Pallas kernels  70.3 us (97%)
  local copies, waits for them, and re-layouts  1.77 us (2%)
    pallas_call x1, Pallas kernels, local(): pl.pallas_call(functools.partial(moe_kernel, experts, chips), out_shape=j...  70.3 us
    unnamed x1, local copies, waits for them, and re-layouts  1.77 us

profile of v2, /device:TPU:0, one launch (start us, length us, event | category | flops | bytes accessed | tf_op | source)
XLA Modules:
  0.0 72.1 jit_solution(11177024842361872557)
XLA Ops:
  0.0 70.3 %shard_map.64 = bf16[64,3072]{1,0:T(8,128)(2,1)} custom-call(bf16[64,3072]{1,0:T(8,128)(2,1)} %tokens.1, s32[2,64]{1,0:T(2,128)} %bitcast.3, bf16[4,3072]{1,0:T(4,128)(2,1)} %bitcast.2, bf16[3072,2048]{1,0:T(8,128)(2,1)} %wg_hbm.1, bf16[3072,2048]{1,0:T(8,128)(2,1)} %wu_hbm.1, bf16[2048,3072]{1,0:T(8,128)(2,1)} %wd_hbm.1), custom_call_target="tpu_custom_call" | custom-call | flops 21743271936 | bytes 37748736 | tf_op jit(solution)/shard_map/pallas_call | solution.py:323
  70.3 1.8 %copy.8 = bf16[64,3072]{1,0:T(8,128)(2,1)} copy(bf16[64,3072]{1,0:T(8,128)(2,1)} %shard_map.64) | data formatting | bytes 786432

commit v3 on v2

--- a/solution.py
+++ b/solution.py
@@ -262,14 +262,16 @@
     spread(1)
     for s in range(experts):
         hidden_units(s, 0, 1)
-        if s >= 1:
+        if s >= 2:
             across(s - 1)
-        if s >= 2:
+        if s >= 3:
             home(s - 2)
         if steps > 1:
             hidden_units(s, 1, steps)
         if s + 1 < experts:
             forward(s + 1)
+        if s == max(1, experts - 2):
+            across(0)
         down(s)
         pair(s)
         if s + 3 < experts:
@@ -278,6 +280,7 @@
             spread(s + 2)
     home(experts - 2)
     across(experts - 1)
+    home(0)
 
     logits = lax.dot_general(router[...], tokens[...], (((1,), (1,)), ((), ())), preferred_element_type=f32)
     gap = jnp.sum(jnp.where(expert_row == first, logits, 0.0) - jnp.where(expert_row == second, logits, 0.0),

time: 72.2 us -> 72.8 us (level)
  no operation moved by 1% of the time
where the time goes in v3:
time: 72.8 us; the launch traced here: 72.7 us
  Pallas kernels  70.9 us (97%)
  local copies, waits for them, and re-layouts  1.77 us (2%)
    pallas_call x1, Pallas kernels, local(): pl.pallas_call(functools.partial(moe_kernel, experts, chips), out_shape=j...  70.9 us
    unnamed x1, local copies, waits for them, and re-layouts  1.77 us

profile of v3, /device:TPU:0, one launch (start us, length us, event | category | flops | bytes accessed | tf_op | source)
XLA Modules:
  0.0 72.7 jit_solution(4320996937780770913)
XLA Ops:
  0.0 70.9 %shard_map.64 = bf16[64,3072]{1,0:T(8,128)(2,1)} custom-call(bf16[64,3072]{1,0:T(8,128)(2,1)} %tokens.1, s32[2,64]{1,0:T(2,128)} %bitcast.3, bf16[4,3072]{1,0:T(4,128)(2,1)} %bitcast.2, bf16[3072,2048]{1,0:T(8,128)(2,1)} %wg_hbm.1, bf16[3072,2048]{1,0:T(8,128)(2,1)} %wu_hbm.1, bf16[2048,3072]{1,0:T(8,128)(2,1)} %wd_hbm.1), custom_call_target="tpu_custom_call" | custom-call | flops 21743271936 | bytes 37748736 | tf_op jit(solution)/shard_map/pallas_call | solution.py:326
  70.9 1.8 %copy.8 = bf16[64,3072]{1,0:T(8,128)(2,1)} copy(bf16[64,3072]{1,0:T(8,128)(2,1)} %shard_map.64) | data formatting | bytes 786432
